TPU v7x, 32 devices: a whole 2x2x4 slice. The times are simulated.
32 devices in a mesh: parts: 2 (over x), space: 16 (over z, y, core).
Axes of the slice: x: 2, y: 2, z: 4, core: 2. Of those that a mesh axis runs over, the one named last changes fastest.
Arguments:
- gas_q: bfloat16 [12288, 512], P(('parts', 'space')), parts along dimension 0, may hold values from -6 to 6
- gas_k: bfloat16 [12288, 512], P(('parts', 'space')), parts along dimension 0, may hold values from -6 to 6
- gas_v: bfloat16 [12288, 512], P(('parts', 'space')), parts along dimension 0, may hold values from -6 to 6
- gas_cotan: bfloat16 [12288, 512], P(('parts', 'space')), parts along dimension 0, may hold values from -6 to 6
- nbr_ids: int32 [96, 16], P('parts'), parts along dimension 0, may hold values from 0 to 47, as said below
- nbr_valid: int32 [96, 16], P('parts'), parts along dimension 0, may hold values from 0 to 1
- if_row: int32 [512], P(('parts', 'space')), parts along dimension 0, may hold values from 0 to 383, as said below
- if_dst: int32 [512], P(('parts', 'space')), parts along dimension 0, may hold values from 0 to 15, as said below
- melt_q: bfloat16 [4096, 512], P(('parts', 'space')), parts along dimension 0, may hold values from -6 to 6
- melt_k: bfloat16 [4096, 512], P(('parts', 'space')), parts along dimension 0, may hold values from -6 to 6
- melt_v: bfloat16 [4096, 512], P(('parts', 'space')), parts along dimension 0, may hold values from -6 to 6
- melt_cotan: bfloat16 [4096, 512], P(('parts', 'space')), parts along dimension 0, may hold values from -6 to 6
Outputs:
- gas_out: bfloat16 [12288, 512], P(('parts', 'space')), parts along dimension 0
- gas_dq: bfloat16 [12288, 512], P(('parts', 'space')), parts along dimension 0
- gas_dk: bfloat16 [12288, 512], P(('parts', 'space')), parts along dimension 0
- gas_dv: bfloat16 [12288, 512], P(('parts', 'space')), parts along dimension 0
- melt_out: bfloat16 [4096, 512], P(('parts', 'space')), parts along dimension 0
- melt_dq: bfloat16 [4096, 512], P(('parts', 'space')), parts along dimension 0
- melt_dk: bfloat16 [4096, 512], P(('parts', 'space')), parts along dimension 0
- melt_dv: bfloat16 [4096, 512], P(('parts', 'space')), parts along dimension 0
There are 2 independent parts, one for each index of `parts`. A program takes and returns all parts, laid end to end along the dimension named above; each array names one. Nothing has to cross between parts.
Inputs may be any that keep to these rules, and one draw needn't show every extreme that they name: `nbr_ids`: for every gas block b the live entries of row b name distinct blocks, b itself among them, all in gas groups within 3 of b's group. For two different gas groups r and o within 3 of each other, the live entries of the blocks of group r name exactly one block of group o. Entries that are not live name any block. `if_row`: the 16 entries of one gas group are distinct. `if_dst`: the 16 entries of one gas group name 8 melt groups, 2 entries each; some melt group is named 2 times by every gas group.
All inputs are finite; a program needn't handle non-finite values.
Results may differ from a plain program's by a relative error of at most 0.012.
The roundings to bfloat16 on the way count: a program that leaves them out, or rounds other values in their place, can miss the bound.
Values may be sent and summed in bfloat16 or wider, within the bound.
A program may use at most 128 MiB of HBM per device.

v0:
```python
import math
import jax
import jax.numpy as jnp
from jax import lax
from jax.sharding import PartitionSpec as P

HEADS = 8
HEAD_DIM = 64
BLK = 128
WIN = 3
ICAP = 2
GB_DEV = 3
MASKED_SCORE = -1e30


def shifted_2(value, axis, steps):
    count = lax.axis_size(axis)
    initial, last = (max(0, -steps), min(count, count - steps))
    return lax.ppermute(value, axis, [(source, source + steps) for source in range(initial, last)])


def attend(queries, key_rows, values, cotangent, key_mask):
    row_count = queries.shape[0]
    key_count = key_rows.shape[0]
    query_heads = queries.reshape(row_count, HEADS, HEAD_DIM)
    key_heads = key_rows.reshape(key_count, HEADS, HEAD_DIM)
    value_heads = values.reshape(key_count, HEADS, HEAD_DIM)
    cot_heads = cotangent.reshape(row_count, HEADS, HEAD_DIM)
    inv_root = 1.0 / math.sqrt(HEAD_DIM)
    wide = jnp.float32
    scores = (
        jnp.einsum("rhd,shd->hrs", query_heads, key_heads, preferred_element_type=wide) * inv_root
    )
    scores = jnp.where(key_mask[None, None, :], scores, MASKED_SCORE)
    row_max = jnp.max(scores, axis=2, keepdims=True)
    shifted = jnp.exp(scores - row_max)
    weights = shifted / jnp.sum(shifted, axis=2, keepdims=True)
    weights_low = weights.astype(jnp.bfloat16)
    attended = jnp.einsum(
        "hrs,shd->rhd", weights_low, value_heads, preferred_element_type=wide
    ).reshape(row_count, -1)
    grad_weights = jnp.einsum("rhd,shd->hrs", cot_heads, value_heads, preferred_element_type=wide)
    row_delta = jnp.sum(weights * grad_weights, axis=2, keepdims=True)
    dscore = (weights * (grad_weights - row_delta)).astype(jnp.bfloat16)
    grad_query = (
        jnp.einsum("hrs,shd->rhd", dscore, key_heads, preferred_element_type=wide).reshape(
            row_count, -1
        )
        * inv_root
    )
    grad_key = (
        jnp.einsum("hrs,rhd->shd", dscore, query_heads, preferred_element_type=wide).reshape(
            key_count, -1
        )
        * inv_root
    )
    grad_value = jnp.einsum(
        "hrs,rhd->shd", weights_low, cot_heads, preferred_element_type=wide
    ).reshape(key_count, -1)
    return (attended, grad_query, grad_key, grad_value)


def local(
    gas_q,
    gas_k,
    gas_v,
    gas_cotan,
    nbr_ids,
    nbr_valid,
    if_row,
    if_dst,
    melt_q,
    melt_k,
    melt_v,
    melt_cotan,
):
    myself = lax.axis_index("space")
    devices = lax.axis_size("space")
    width = gas_q.shape[1]
    kv_local = jnp.stack([gas_k.reshape(GB_DEV, BLK, width), gas_v.reshape(GB_DEV, BLK, width)])
    offsets = [o for o in range(-WIN, WIN + 1) if o != 0]
    arrived_list = []
    arrived_ids = [myself * GB_DEV + jnp.arange(GB_DEV, dtype=jnp.int32)]
    for offset in offsets:
        owner_dev = myself - offset
        arrived = shifted_2(kv_local, "space", offset)
        arrived_list.append(arrived)
        present = (owner_dev >= 0) & (owner_dev < devices)
        arrived_ids.append(
            jnp.where(present, owner_dev * GB_DEV + jnp.arange(GB_DEV, dtype=jnp.int32), -1)
        )
    available = jnp.concatenate([kv_local] + arrived_list, axis=1)
    available_ids = jnp.concatenate(arrived_ids)
    slot_count = available.shape[1]
    my_ids = lax.dynamic_slice_in_dim(nbr_ids, myself * GB_DEV, GB_DEV, 0)
    my_live = lax.dynamic_slice_in_dim(nbr_valid, myself * GB_DEV, GB_DEV, 0) == 1
    matches = my_ids[:, :, None] == available_ids[None, None, :]
    present_entry = jnp.any(matches, axis=2) & my_live
    slot_index = jnp.sum(jnp.where(matches, jnp.arange(slot_count), 0), axis=2)
    query_blocks = gas_q.reshape(GB_DEV, BLK, width)
    cot_blocks = gas_cotan.reshape(GB_DEV, BLK, width)

    def gas_block(grad_slots, inputs_block):
        query_rows, cot_rows, slot_row, entry_ok = inputs_block
        list_len = slot_row.shape[0]
        key_rows = jnp.take(available[0], slot_row, axis=0).reshape(list_len * BLK, width)
        value_rows = jnp.take(available[1], slot_row, axis=0).reshape(list_len * BLK, width)
        key_mask = jnp.repeat(entry_ok, BLK)
        attended, grad_query, grad_key, grad_value = attend(
            query_rows, key_rows, value_rows, cot_rows, key_mask
        )
        grad_pair = jnp.stack(
            [grad_key.reshape(list_len, BLK, width), grad_value.reshape(list_len, BLK, width)]
        )
        grad_pair = jnp.where(entry_ok[None, :, None, None], grad_pair, 0.0)
        grad_slots = grad_slots.at[:, slot_row].add(grad_pair)
        return (grad_slots, (attended.astype(jnp.bfloat16), grad_query.astype(jnp.bfloat16)))

    start_slots = jnp.zeros((2, slot_count, BLK, width), jnp.float32)
    grad_slots, (gas_att, gas_gq) = lax.scan(
        gas_block, start_slots, (query_blocks, cot_blocks, slot_index, present_entry)
    )
    own_grads = grad_slots[:, :GB_DEV]
    for number, offset in enumerate(offsets):
        outgoing = grad_slots[:, GB_DEV + number * GB_DEV : GB_DEV + (number + 1) * GB_DEV]
        returned = shifted_2(outgoing, "space", -offset)
        own_grads = own_grads + returned
    if_count = if_row.shape[0]
    entry_index = jnp.arange(if_count)
    earlier = entry_index[None, :] < entry_index[:, None]
    slot_rank = jnp.sum((if_dst[:, None] == if_dst[None, :]) & earlier, axis=1)
    slot_place = if_dst * ICAP + slot_rank
    send_keys = (
        jnp.zeros((devices * ICAP, width), jnp.bfloat16)
        .at[slot_place]
        .set(gas_k[if_row])
        .reshape(devices, ICAP, width)
    )
    send_values = (
        jnp.zeros((devices * ICAP, width), jnp.bfloat16)
        .at[slot_place]
        .set(gas_v[if_row])
        .reshape(devices, ICAP, width)
    )
    row_flag = (
        jnp.zeros((devices * ICAP,), jnp.bfloat16).at[slot_place].set(1.0).reshape(devices, ICAP)
    )
    recv_keys, recv_values, recv_flag = (
        lax.all_to_all(send_keys, "space", split_axis=0, concat_axis=0, tiled=True),
        lax.all_to_all(send_values, "space", split_axis=0, concat_axis=0, tiled=True),
        lax.all_to_all(row_flag, "space", split_axis=0, concat_axis=0, tiled=True),
    )
    melt_rows = melt_q.shape[0]
    key_rows = jnp.concatenate([melt_k, recv_keys.reshape(-1, width)], axis=0)
    value_rows = jnp.concatenate([melt_v, recv_values.reshape(-1, width)], axis=0)
    key_mask = jnp.concatenate([jnp.ones((melt_rows,), bool), recv_flag.reshape(-1) > 0])
    melt_att, melt_gq, melt_gk, melt_gv = attend(melt_q, key_rows, value_rows, melt_cotan, key_mask)
    back_keys, back_values = (
        lax.all_to_all(
            melt_gk[melt_rows:].reshape(devices, ICAP, width),
            "space",
            split_axis=0,
            concat_axis=0,
            tiled=True,
        ),
        lax.all_to_all(
            melt_gv[melt_rows:].reshape(devices, ICAP, width),
            "space",
            split_axis=0,
            concat_axis=0,
            tiled=True,
        ),
    )
    extra_keys = back_keys.reshape(-1, width)[slot_place]
    extra_values = back_values.reshape(-1, width)[slot_place]
    key_flat = own_grads[0].reshape(-1, width).at[if_row].add(extra_keys)
    value_flat = own_grads[1].reshape(-1, width).at[if_row].add(extra_values)
    low = jnp.bfloat16
    return (
        gas_att.reshape(-1, width),
        gas_gq.reshape(-1, width),
        key_flat.astype(low),
        value_flat.astype(low),
        melt_att.astype(low),
        melt_gq.astype(low),
        melt_gk[:melt_rows].astype(low),
        melt_gv[:melt_rows].astype(low),
    )


def solution(mesh):
    in_specs = (
        P(("parts", "space"), None),
        P(("parts", "space"), None),
        P(("parts", "space"), None),
        P(("parts", "space"), None),
        P("parts", None),
        P("parts", None),
        P(("parts", "space")),
        P(("parts", "space")),
        P(("parts", "space"), None),
        P(("parts", "space"), None),
        P(("parts", "space"), None),
        P(("parts", "space"), None),
    )
    out_specs = (
        P(("parts", "space"), None),
        P(("parts", "space"), None),
        P(("parts", "space"), None),
        P(("parts", "space"), None),
        P(("parts", "space"), None),
        P(("parts", "space"), None),
        P(("parts", "space"), None),
        P(("parts", "space"), None),
    )
    return jax.shard_map(local, mesh=mesh, in_specs=in_specs, out_specs=out_specs, check_vma=False)
```

profile of v0, /device:TPU:0, one launch (start us, length us, event | category | flops | bytes accessed | tf_op | source)
XLA Modules:
  0.0 591.5 jit_solution(17577238697560599775)
XLA Ops:
  10.1 5.5 collective-permute-start.4
  16.9 6.7 %collective-permute-done = bf16[2,3,128,512]{3,2,1,0:T(8,128)(2,1)} collective-permute-done((bf16[2,3,128,512]{3,2,1,0:T(8,128)(2,1)}, bf16[2,3,128,512]{3,2,1,0:T(8,128)(2,1)}, u32[]{:S(2)}, u32[]{:S(2)}) %collective-permute-start) | collective-permute-done | bytes 786464 | tf_op jit(solution)/shard_map/ppermute | solution.py:19
  31.0 32.9 %collective-permute-done.4 = bf16[2,3,128,512]{3,2,1,0:T(8,128)(2,1)S(1)} collective-permute-done((bf16[2,3,128,512]{3,2,1,0:T(8,128)(2,1)}, bf16[2,3,128,512]{3,2,1,0:T(8,128)(2,1)S(1)}, u32[]{:S(2)}, u32[]{:S(2)}) %collective-permute-start.4) | collective-permute-done | bytes 786464 | tf_op jit(solution)/shard_map/ppermute | solution.py:19
  64.8 14.4 %collective-permute-done.5 = bf16[2,3,128,512]{3,2,1,0:T(8,128)(2,1)} collective-permute-done((bf16[2,3,128,512]{3,2,1,0:T(8,128)(2,1)}, bf16[2,3,128,512]{3,2,1,0:T(8,128)(2,1)}, u32[]{:S(2)}, u32[]{:S(2)}) %collective-permute-start.5) | collective-permute-done | bytes 786464 | tf_op jit(solution)/shard_map/ppermute | solution.py:19
  81.3 5.6 broadcast_in_dim.104
  86.9 311.6 %while.14 = (s32[]{:T(128)}, f32[2,21,128,512]{3,2,1,0:T(8,128)}, bf16[3,128,512]{2,1,0:T(8,128)(2,1)}, bf16[3,128,512]{2,1,0:T(8,128)(2,1)}, s32[3,16]{1,0:T(4,...) while((s32[]{:T(128)}, f32[2,21,128,512]{3,2,1,0:T(8,128)}, ...), condition=%wide.region_7.9_spmd, body=%wide.region_2.8_spmd.sunk | while | flops 1651705984 | bytes 253007152 | solution.py:120
  86.9 4.8 slice_bitcast_fusion.3
  108.7 4.7 fusion.106
  113.4 4.5 copy.134
  118.0 4.2 reshape.361
  123.2 5.6 multiply_reduce_fusion.3
  134.5 5.7 fusion.110
  146.9 5.3 copy.136
  152.1 4.2 fusion.107
  159.3 5.3 copy.133
  164.6 8.5 %fusion.108 = f32[16,2,128,512]{3,2,1,0:T(8,128)} fusion(f32[1,16,128,512]{3,2,0,1:T(8,128)} %copy.133, f32[1,16,128,512]{3,2,0,1:T(8,128)} %copy.136, pred[16]{0:T(512)(128)(4,1)S(1)} %dynamic-slice_bitcast_fusion.2), kind=kLoop, calls=%fused_computation.14.clone.1 | loop fusion | flops 4194304 | bytes 16777232 | tf_op jit(solution)/shard_map/while/body/eval_jaxpr/jit(_where)/select_n | solution.py:115
  173.0 17.9 %scatter_fusion = f32[2,21,128,512]{3,2,1,0:T(8,128)} fusion(f32[2,21,128,512]{3,2,1,0:T(8,128)} %get-tuple-element.264, s32[16]{0:T(128)S(1)} %fusion.105, f32[16,2,128,512]{3,2,1,0:T(8,128)} %fusion.108), kind=kCustom, calls=%fused_computation.6.clone.1 | custom fusion | flops 2097152 | bytes 25165888 | tf_op jit(solution)/shard_map/while/body/eval_jaxpr/scatter-add | solution.py:116
  191.0 4.8 slice_bitcast_fusion.3
  212.8 4.7 fusion.106
  217.5 4.5 copy.134
  222.0 4.2 reshape.361
  227.3 5.6 multiply_reduce_fusion.3
  238.6 5.7 fusion.110
  251.0 5.3 copy.136
  256.2 4.2 fusion.107
  263.4 5.3 copy.133
  268.6 8.5 %fusion.108 = f32[16,2,128,512]{3,2,1,0:T(8,128)} fusion(f32[1,16,128,512]{3,2,0,1:T(8,128)} %copy.133, f32[1,16,128,512]{3,2,0,1:T(8,128)} %copy.136, pred[16]{0:T(512)(128)(4,1)S(1)} %dynamic-slice_bitcast_fusion.2), kind=kLoop, calls=%fused_computation.14.clone.1 | loop fusion | flops 4194304 | bytes 16777232 | tf_op jit(solution)/shard_map/while/body/eval_jaxpr/jit(_where)/select_n | solution.py:115
  277.1 17.7 %scatter_fusion = f32[2,21,128,512]{3,2,1,0:T(8,128)} fusion(f32[2,21,128,512]{3,2,1,0:T(8,128)} %get-tuple-element.264, s32[16]{0:T(128)S(1)} %fusion.105, f32[16,2,128,512]{3,2,1,0:T(8,128)} %fusion.108), kind=kCustom, calls=%fused_computation.6.clone.1 | custom fusion | flops 2097152 | bytes 25165888 | tf_op jit(solution)/shard_map/while/body/eval_jaxpr/scatter-add | solution.py:116
  294.8 4.8 slice_bitcast_fusion.3
  316.6 4.7 fusion.106
  321.3 4.5 copy.134
  325.9 4.2 reshape.361
  331.1 5.6 multiply_reduce_fusion.3
  342.4 5.7 fusion.110
  354.8 5.3 copy.136
  367.2 5.3 copy.133
  372.5 8.5 %fusion.108 = f32[16,2,128,512]{3,2,1,0:T(8,128)} fusion(f32[1,16,128,512]{3,2,0,1:T(8,128)} %copy.133, f32[1,16,128,512]{3,2,0,1:T(8,128)} %copy.136, pred[16]{0:T(512)(128)(4,1)S(1)} %dynamic-slice_bitcast_fusion.2), kind=kLoop, calls=%fused_computation.14.clone.1 | loop fusion | flops 4194304 | bytes 16777232 | tf_op jit(solution)/shard_map/while/body/eval_jaxpr/jit(_where)/select_n | solution.py:115
  380.9 17.5 %scatter_fusion = f32[2,21,128,512]{3,2,1,0:T(8,128)} fusion(f32[2,21,128,512]{3,2,1,0:T(8,128)} %get-tuple-element.264, s32[16]{0:T(128)S(1)} %fusion.105, f32[16,2,128,512]{3,2,1,0:T(8,128)} %fusion.108), kind=kCustom, calls=%fused_computation.6.clone.1 | custom fusion | flops 2097152 | bytes 25165888 | tf_op jit(solution)/shard_map/while/body/eval_jaxpr/scatter-add | solution.py:116
  398.5 7.4 %fusion.52 = (f32[2,3,128,512]{3,2,1,0:T(8,128)}, f32[2,3,128,512]{3,2,1,0:T(8,128)}, f32[2,3,128,512]{3,2,1,0:T(8,128)}, f32[2,3,128,512]{3,2,1,0:T(8,128)S(1)}...) fusion(f32[2,21,128,512]{3,2,1,0:T(8,128)} %get-tuple-element.60), kind=kLoop, calls=%fused_computation.124 | loop fusion | bytes 18874368 | tf_op jit(solution)/shard_map/slice | solution.py:125
  408.8 9.8 %all-to-all-start = ((bf16[16,1,2]{2,1,0:T(2,128)(2,1)}), bf16[16,1,2]{2,1,0:T(2,128)(2,1)S(1)}, u32[]{:S(2)}, u32[]{:S(2)}) async-start(bf16[16,1,2]{2,1,0:T(2,128)(2,1)} %all_to_all.24), calls=%async_computation | async-start | bytes 16384 | tf_op jit(solution)/shard_map/all_to_all | solution.py:151
  429.8 18.1 %all-to-all-done = bf16[16,1,2]{2,1,0:T(2,128)(2,1)S(1)} async-done(((bf16[16,1,2]{2,1,0:T(2,128)(2,1)}), bf16[16,1,2]{2,1,0:T(2,128)(2,1)S(1)}, u32[]{:S(2)}, u32[]{:S(2)}) %all-to-all-start) | async-done | bytes 96 | tf_op jit(solution)/shard_map/all_to_all | solution.py:151
  451.6 6.4 %all-to-all-done.1 = bf16[16,2,512]{2,1,0:T(2,128)(2,1)S(1)} async-done(((bf16[16,2,512]{2,1,0:T(2,128)(2,1)}), bf16[16,2,512]{2,1,0:T(2,128)(2,1)S(1)}, u32[]{:S(2)}, u32[]{:S(2)}) %all-to-all-start.1) | async-done | bytes 32800 | tf_op jit(solution)/shard_map/all_to_all | solution.py:149
  463.1 5.5 collective-permute-start.6
  468.6 5.8 collective-permute-start.7
  495.9 5.4 all-to-all-start.3
  509.8 58.3 %all-to-all-done.3 = f32[16,2,512]{2,1,0:T(2,128)S(1)} async-done(((f32[16,2,512]{2,1,0:T(2,128)}), f32[16,2,512]{2,1,0:T(2,128)S(1)}, u32[]{:S(2)}, u32[]{:S(2)}) %all-to-all-start.3) | async-done | bytes 65568 | tf_op jit(solution)/shard_map/all_to_all | solution.py:159
  568.2 7.4 %all-to-all-start.4 = ((f32[16,2,512]{2,1,0:T(2,128)}), f32[16,2,512]{2,1,0:T(2,128)S(1)}, u32[]{:S(2)}, u32[]{:S(2)}) async-start(f32[16,2,512]{2,1,0:T(2,128)} %reshape.206), calls=%async_computation.4 | async-start | bytes 131072 | tf_op jit(solution)/shard_map/all_to_all | solution.py:166
  582.6 5.1 add_add_fusion
  (196 shorter events, 188.7 us)
Async XLA Ops:
  3.1 20.5 %collective-permute-start = (bf16[2,3,128,512]{3,2,1,0:T(8,128)(2,1)}, bf16[2,3,128,512]{3,2,1,0:T(8,128)(2,1)}, u32[]{:S(2)}, u32[]{:S(2)}) collective-permute-start(bf16[2,3,128,512]{3,2,1,0:T(8,128)(2,1)} %get-tuple-element.158), channel_id=1, source_target_pairs={{3,0},{4,1},{5,2},{6,3},{7,4},{8,5},{9,6},{10,7},{11,8},{12,9},{13... | collective-permute-start | bytes 2359304 | tf_op jit(solution)/shard_map/ppermute | solution.py:19
  4.4 23.7 %collective-permute-start.1 = (bf16[2,3,128,512]{3,2,1,0:T(8,128)(2,1)}, bf16[2,3,128,512]{3,2,1,0:T(8,128)(2,1)S(1)}, u32[]{:S(2)}, u32[]{:S(2)}) collective-permute-start(bf16[2,3,128,512]{3,2,1,0:T(8,128)(2,1)} %get-tuple-element.158), channel_id=1, source_target_pairs={{2,0},{3,1},{4,2},{5,3},{6,4},{7,5},{8,6},{9,7},{10,8},{11,9},{12,... | collective-permute-start | bytes 2359304 | tf_op jit(solution)/shard_map/ppermute | solution.py:19
  5.7 23.4 %collective-permute-start.2 = (bf16[2,3,128,512]{3,2,1,0:T(8,128)(2,1)}, bf16[2,3,128,512]{3,2,1,0:T(8,128)(2,1)S(1)}, u32[]{:S(2)}, u32[]{:S(2)}) collective-permute-start(bf16[2,3,128,512]{3,2,1,0:T(8,128)(2,1)} %get-tuple-element.158), channel_id=1, source_target_pairs={{1,0},{2,1},{3,2},{4,3},{5,4},{6,5},{7,6},{8,7},{9,8},{10,9},{11,1... | collective-permute-start | bytes 2359304 | tf_op jit(solution)/shard_map/ppermute | solution.py:19
  7.0 23.0 %collective-permute-start.3 = (bf16[2,3,128,512]{3,2,1,0:T(8,128)(2,1)}, bf16[2,3,128,512]{3,2,1,0:T(8,128)(2,1)S(1)}, u32[]{:S(2)}, u32[]{:S(2)}) collective-permute-start(bf16[2,3,128,512]{3,2,1,0:T(8,128)(2,1)} %get-tuple-element.158), channel_id=1, source_target_pairs={{0,1},{1,2},{2,3},{3,4},{4,5},{5,6},{6,7},{7,8},{8,9},{9,10},{10,1... | collective-permute-start | bytes 2359304 | tf_op jit(solution)/shard_map/ppermute | solution.py:19
  10.1 53.8 %collective-permute-start.4 = (bf16[2,3,128,512]{3,2,1,0:T(8,128)(2,1)}, bf16[2,3,128,512]{3,2,1,0:T(8,128)(2,1)S(1)}, u32[]{:S(2)}, u32[]{:S(2)}) collective-permute-start(bf16[2,3,128,512]{3,2,1,0:T(8,128)(2,1)} %get-tuple-element.158), channel_id=1, source_target_pairs={{0,2},{1,3},{2,4},{3,5},{4,6},{5,7},{6,8},{7,9},{8,10},{9,11},{10,... | collective-permute-start | bytes 2359304 | tf_op jit(solution)/shard_map/ppermute | solution.py:19
  23.6 55.6 %collective-permute-start.5 = (bf16[2,3,128,512]{3,2,1,0:T(8,128)(2,1)}, bf16[2,3,128,512]{3,2,1,0:T(8,128)(2,1)}, u32[]{:S(2)}, u32[]{:S(2)}) collective-permute-start(bf16[2,3,128,512]{3,2,1,0:T(8,128)(2,1)} %get-tuple-element.158), channel_id=1, source_target_pairs={{0,3},{1,4},{2,5},{3,6},{4,7},{5,8},{6,9},{7,10},{8,11},{9,12},{10... | collective-permute-start | bytes 2359304 | tf_op jit(solution)/shard_map/ppermute | solution.py:19
  123.2 5.6 slice-start
  123.2 6.5 %slice-start.1 = ((s8[8388608]{0:T(1024)(128)(4,1)}), s8[4194304]{0:T(1024)(128)(4,1)S(1)}, s32[]{:S(2)}) async-start(s8[8388608]{0:T(1024)(128)(4,1)} %bitcast.156), calls=%async_computation.6 | async-start | bytes 8388608 | tf_op jit(solution)/shard_map/while
  130.8 2.0 copy-start
  227.3 5.6 slice-start
  227.3 6.5 %slice-start.1 = ((s8[8388608]{0:T(1024)(128)(4,1)}), s8[4194304]{0:T(1024)(128)(4,1)S(1)}, s32[]{:S(2)}) async-start(s8[8388608]{0:T(1024)(128)(4,1)} %bitcast.156), calls=%async_computation.6 | async-start | bytes 8388608 | tf_op jit(solution)/shard_map/while
  234.9 2.0 copy-start
  331.1 5.6 slice-start
  331.1 6.5 %slice-start.1 = ((s8[8388608]{0:T(1024)(128)(4,1)}), s8[4194304]{0:T(1024)(128)(4,1)S(1)}, s32[]{:S(2)}) async-start(s8[8388608]{0:T(1024)(128)(4,1)} %bitcast.156), calls=%async_computation.6 | async-start | bytes 8388608 | tf_op jit(solution)/shard_map/while
  338.7 2.0 copy-start
  398.5 8.7 %copy-start.8 = (s32[16]{0:T(128)S(1)}, s32[16]{0:T(128)}, u32[]{:S(2)}) copy-start(s32[16]{0:T(128)} %param.23) | copy-start | bytes 196
  398.5 8.9 %copy-start.9 = (s32[16]{0:T(128)S(1)}, s32[16]{0:T(128)}, u32[]{:S(2)}) copy-start(s32[16]{0:T(128)} %param.22) | copy-start | bytes 196
  398.5 26.0 %copy-start.4 = (bf16[128,512]{1,0:T(8,128)(2,1)S(1)}, bf16[128,512]{1,0:T(8,128)(2,1)}, u32[]{:S(2)}) copy-start(bf16[128,512]{1,0:T(8,128)(2,1)} %param.25) | copy-start | bytes 393220
  398.5 26.7 %copy-start.5 = (bf16[128,512]{1,0:T(8,128)(2,1)S(1)}, bf16[128,512]{1,0:T(8,128)(2,1)}, u32[]{:S(2)}) copy-start(bf16[128,512]{1,0:T(8,128)(2,1)} %param.24) | copy-start | bytes 393220
  398.5 28.3 %copy-start.6 = (bf16[128,512]{1,0:T(8,128)(2,1)S(1)}, bf16[128,512]{1,0:T(8,128)(2,1)}, u32[]{:S(2)}) copy-start(bf16[128,512]{1,0:T(8,128)(2,1)} %param.26) | copy-start | bytes 393220
  405.9 71.0 %collective-permute-start.10 = (f32[2,3,128,512]{3,2,1,0:T(8,128)}, f32[2,3,128,512]{3,2,1,0:T(8,128)S(1)}, u32[]{:S(2)}, u32[]{:S(2)}) collective-permute-start(f32[2,3,128,512]{3,2,1,0:T(8,128)} %get-tuple-element.152), channel_id=1, source_target_pairs={{2,0},{3,1},{4,2},{5,3},{6,4},{7,5},{8,6},{9,7},{10,8},{11,9},{12,... | collective-permute-start | bytes 4718600 | tf_op jit(solution)/shard_map/ppermute | solution.py:19
  407.4 1.4 copy-start.7
  408.8 39.2 %all-to-all-start = ((bf16[16,1,2]{2,1,0:T(2,128)(2,1)}), bf16[16,1,2]{2,1,0:T(2,128)(2,1)S(1)}, u32[]{:S(2)}, u32[]{:S(2)}) async-start(bf16[16,1,2]{2,1,0:T(2,128)(2,1)} %all_to_all.24), calls=%async_computation | async-start | bytes 16384 | tf_op jit(solution)/shard_map/all_to_all | solution.py:151
  425.3 57.5 %copy-start.1 = (bf16[128,512]{0,1:T(8,128)(2,1)}, bf16[128,512]{0,1:T(8,128)(2,1)S(1)}, u32[]{:S(2)}) copy-start(bf16[128,512]{0,1:T(8,128)(2,1)S(1)} %copy.100) | copy-start | bytes 393220
  447.9 10.1 %all-to-all-start.1 = ((bf16[16,2,512]{2,1,0:T(2,128)(2,1)}), bf16[16,2,512]{2,1,0:T(2,128)(2,1)S(1)}, u32[]{:S(2)}, u32[]{:S(2)}) async-start(bf16[16,2,512]{2,1,0:T(2,128)(2,1)} %reshape.200), calls=%async_computation.1 | async-start | bytes 65536 | tf_op jit(solution)/shard_map/all_to_all | solution.py:149
  458.0 22.3 %all-to-all-start.2 = ((bf16[16,2,512]{2,1,0:T(2,128)(2,1)}), bf16[16,2,512]{2,1,0:T(2,128)(2,1)S(1)}, u32[]{:S(2)}, u32[]{:S(2)}) async-start(bf16[16,2,512]{2,1,0:T(2,128)(2,1)} %reshape.202), calls=%async_computation.2 | async-start | bytes 65536 | tf_op jit(solution)/shard_map/all_to_all | solution.py:150
  461.8 21.0 %copy-start.3 = (bf16[32,8,64]{0,2,1:T(8,128)(2,1)}, bf16[32,8,64]{0,2,1:T(8,128)(2,1)S(1)}, u32[]{:S(2)}) copy-start(bf16[32,8,64]{0,2,1:T(8,128)(2,1)S(1)} %copy.99) | copy-start | bytes 98308
  461.8 120.7 %collective-permute-start.11 = (f32[2,3,128,512]{3,2,1,0:T(8,128)}, f32[2,3,128,512]{3,2,1,0:T(8,128)}, u32[]{:S(2)}, u32[]{:S(2)}) collective-permute-start(f32[2,3,128,512]{3,2,1,0:T(8,128)} %get-tuple-element.151), channel_id=1, source_target_pairs={{3,0},{4,1},{5,2},{6,3},{7,4},{8,5},{9,6},{10,7},{11,8},{12,9},{13... | collective-permute-start | bytes 4718600 | tf_op jit(solution)/shard_map/ppermute | solution.py:19
  463.1 119.4 %collective-permute-start.6 = (f32[2,3,128,512]{3,2,1,0:T(8,128)}, f32[2,3,128,512]{3,2,1,0:T(8,128)}, u32[]{:S(2)}, u32[]{:S(2)}) collective-permute-start(f32[2,3,128,512]{3,2,1,0:T(8,128)} %get-tuple-element.150), channel_id=1, source_target_pairs={{0,3},{1,4},{2,5},{3,6},{4,7},{5,8},{6,9},{7,10},{8,11},{9,12},{10... | collective-permute-start | bytes 4718600 | tf_op jit(solution)/shard_map/ppermute | solution.py:19
  468.6 114.0 %collective-permute-start.7 = (f32[2,3,128,512]{3,2,1,0:T(8,128)}, f32[2,3,128,512]{3,2,1,0:T(8,128)}, u32[]{:S(2)}, u32[]{:S(2)}) collective-permute-start(f32[2,3,128,512]{3,2,1,0:T(8,128)} %get-tuple-element.155), channel_id=1, source_target_pairs={{0,2},{1,3},{2,4},{3,5},{4,6},{5,7},{6,8},{7,9},{8,10},{9,11},{10,... | collective-permute-start | bytes 4718600 | tf_op jit(solution)/shard_map/ppermute | solution.py:19
  474.4 108.2 %collective-permute-start.8 = (f32[2,3,128,512]{3,2,1,0:T(8,128)}, f32[2,3,128,512]{3,2,1,0:T(8,128)}, u32[]{:S(2)}, u32[]{:S(2)}) collective-permute-start(f32[2,3,128,512]{3,2,1,0:T(8,128)} %get-tuple-element.154), channel_id=1, source_target_pairs={{0,1},{1,2},{2,3},{3,4},{4,5},{5,6},{6,7},{7,8},{8,9},{9,10},{10,1... | collective-permute-start | bytes 4718600 | tf_op jit(solution)/shard_map/ppermute | solution.py:19
  476.8 105.8 %collective-permute-start.9 = (f32[2,3,128,512]{3,2,1,0:T(8,128)S(1)}, f32[2,3,128,512]{3,2,1,0:T(8,128)}, u32[]{:S(2)}, u32[]{:S(2)}) collective-permute-start(f32[2,3,128,512]{3,2,1,0:T(8,128)S(1)} %get-tuple-element.153), channel_id=1, source_target_pairs={{1,0},{2,1},{3,2},{4,3},{5,4},{6,5},{7,6},{8,7},{9,8},{10,9},{11,1... | collective-permute-start | bytes 4718600 | tf_op jit(solution)/shard_map/ppermute | solution.py:19
  495.9 72.3 %all-to-all-start.3 = ((f32[16,2,512]{2,1,0:T(2,128)}), f32[16,2,512]{2,1,0:T(2,128)S(1)}, u32[]{:S(2)}, u32[]{:S(2)}) async-start(f32[16,2,512]{2,1,0:T(2,128)} %reshape.204), calls=%async_computation.3 | async-start | bytes 131072 | tf_op jit(solution)/shard_map/all_to_all | solution.py:159
  506.5 71.6 %copy-start.2 = (bf16[128,8,64]{0,2,1:T(8,128)(2,1)S(1)}, bf16[128,8,64]{0,2,1:T(8,128)(2,1)}, u32[]{:S(2)}) copy-start(bf16[128,8,64]{0,2,1:T(8,128)(2,1)} %slice.95) | copy-start | bytes 393220
  568.2 14.3 %all-to-all-start.4 = ((f32[16,2,512]{2,1,0:T(2,128)}), f32[16,2,512]{2,1,0:T(2,128)S(1)}, u32[]{:S(2)}, u32[]{:S(2)}) async-start(f32[16,2,512]{2,1,0:T(2,128)} %reshape.206), calls=%async_computation.4 | async-start | bytes 131072 | tf_op jit(solution)/shard_map/all_to_all | solution.py:166
where the time goes:
time: 595 us; the launch traced here: 592 us
  local copies, waits for them, and re-layouts  194 us (33%)
  waiting for transfers between devices  140 us (24%)
  other arithmetic  108 us (18%)
  matrix products  85.4 us (14%)
  starting transfers between devices  61.8 us (10%)
    all_to_all x1, waiting for transfers between devices, local(): lax.all_to_all(melt_gk[melt_rows:].reshape(devices, ICAP, width), 'space'...  58.3 us
    ppermute x12, waiting for transfers between devices, shifted_2(): lax.ppermute(value, axis, [(source, source + steps) for source in range(i...  54 us
    scatter-add x3, other arithmetic, gas_block(): grad_slots = grad_slots.at[:, slot_row].add(grad_pair)  53.2 us
    ppermute x12, starting transfers between devices, shifted_2(): lax.ppermute(value, axis, [(source, source + steps) for source in range(i...  32.2 us
    while x24, local copies, waits for them, and re-layouts  26 us
    select_n x3, other arithmetic, gas_block(): grad_pair = jnp.where(entry_ok[None, :, None, None], grad_pair, 0.0)  25.4 us
    dot_general x4, matrix products, attend(): jnp.einsum('hrs,shd->rhd', weights_low, value_heads, preferred_element_ty...  18.9 us
    dot_general x4, matrix products, attend(): jnp.einsum('rhd,shd->hrs', cot_heads, value_heads, preferred_element_type...  18.4 us
  transfers between devices with their start and end apart: 17, of which 7 were waited for; matrix products, arithmetic and copies ran while one was open for 8% of the time, Pallas kernels for 0%

commit v1 on v0

--- a/solution.py
+++ b/solution.py
@@ -11,6 +11,22 @@
 ICAP = 2
 GB_DEV = 3
 MASKED_SCORE = -1e30
+
+
+def swapped_with_each(x, axis, split, join):
+    ways, here = (lax.axis_size(axis), lax.axis_index(axis))
+    width = x.shape[split] // ways
+    lengths = list(x.shape)
+    lengths[split] = width
+    height = lengths[join]
+    lengths[join] = height * ways
+    full = jnp.zeros(lengths, x.dtype)
+    for mask in range(ways):
+        part = lax.dynamic_slice_in_dim(x, (here ^ mask) * width, width, axis=split)
+        if mask:
+            part = lax.ppermute(part, axis, [(d, d ^ mask) for d in range(ways)])
+        full = lax.dynamic_update_slice_in_dim(full, part, (here ^ mask) * height, axis=join)
+    return full
 
 
 def shifted_2(value, axis, steps):
@@ -148,7 +164,7 @@
     recv_keys, recv_values, recv_flag = (
         lax.all_to_all(send_keys, "space", split_axis=0, concat_axis=0, tiled=True),
         lax.all_to_all(send_values, "space", split_axis=0, concat_axis=0, tiled=True),
-        lax.all_to_all(row_flag, "space", split_axis=0, concat_axis=0, tiled=True),
+        swapped_with_each(row_flag, "space", 0, 0),
     )
     melt_rows = melt_q.shape[0]
     key_rows = jnp.concatenate([melt_k, recv_keys.reshape(-1, width)], axis=0)

time: 595 us -> 608 us (1.022)
  starting transfers between devices: 61.8 us -> 83.2 us
  waiting for transfers between devices: 140 us -> 131 us
    all_to_all x1, waiting for transfers between devices: 58.3 us -> 4.35 us  [local(): lax.all_to_all(melt_gk[melt_rows:].reshape(devices, ICAP, width), 'space'...]
    all_to_all x1, waiting for transfers between devices: 3.58 us -> 56.7 us  [local(): lax.all_to_all(melt_gv[melt_rows:].reshape(devices, ICAP, width), 'space'...]
    ppermute x0 -> x15, starting transfers between devices: none -> 29.1 us  [swapped_with_each(): part = lax.ppermute(part, axis, [(d, d ^ mask) for d in range(ways)])]
    all_to_all x1 -> x0, waiting for transfers between devices: 18.1 us -> none  [local(): lax.all_to_all(row_flag, 'space', split_axis=0, concat_axis=0, tiled=True)]
    ppermute x0 -> x15, waiting for transfers between devices: none -> 16.2 us  [swapped_with_each(): part = lax.ppermute(part, axis, [(d, d ^ mask) for d in range(ways)])]
    all_to_all x1 -> x0, starting transfers between devices: 9.81 us -> none  [local(): lax.all_to_all(row_flag, 'space', split_axis=0, concat_axis=0, tiled=True)]
    all_to_all x1, waiting for transfers between devices: 6.44 us -> 0.01 us  [local(): lax.all_to_all(send_keys, 'space', split_axis=0, concat_axis=0, tiled=True)]
    unnamed x32 -> x26, local copies, waits for them, and re-layouts: 14.2 us -> 16 us
  transfers between devices with their start and end apart: 17 -> 31, of which waited for: 7 -> 8; matrix products, arithmetic and copies ran while one was open for 8% -> 8% of each run, Pallas kernels for 0% -> 0%
where the time goes in v1:
time: 608 us; the launch traced here: 605 us
  local copies, waits for them, and re-layouts  196 us (32%)
  waiting for transfers between devices  131 us (22%)
  other arithmetic  107 us (18%)
  matrix products  85.4 us (14%)
  starting transfers between devices  83.2 us (14%)
    all_to_all x1, waiting for transfers between devices, local(): lax.all_to_all(melt_gv[melt_rows:].reshape(devices, ICAP, width), 'space'...  56.7 us
    ppermute x12, waiting for transfers between devices, shifted_2(): lax.ppermute(value, axis, [(source, source + steps) for source in range(i...  54 us
    scatter-add x3, other arithmetic, gas_block(): grad_slots = grad_slots.at[:, slot_row].add(grad_pair)  52.9 us
    ppermute x12, starting transfers between devices, shifted_2(): lax.ppermute(value, axis, [(source, source + steps) for source in range(i...  32.3 us
    ppermute x15, starting transfers between devices, swapped_with_each(): part = lax.ppermute(part, axis, [(d, d ^ mask) for d in range(ways)])  29.1 us
    while x24, local copies, waits for them, and re-layouts  26 us
    select_n x3, other arithmetic, gas_block(): grad_pair = jnp.where(entry_ok[None, :, None, None], grad_pair, 0.0)  25.5 us
    dot_general x4, matrix products, attend(): jnp.einsum('hrs,shd->rhd', weights_low, value_heads, preferred_element_ty...  19 us
  transfers between devices with their start and end apart: 31, of which 8 were waited for; matrix products, arithmetic and copies ran while one was open for 8% of the time, Pallas kernels for 0%

profile of v1, /device:TPU:0, one launch (start us, length us, event | category | flops | bytes accessed | tf_op | source)
XLA Modules:
  0.0 604.9 jit_solution(5298020214742970442)
XLA Ops:
  10.1 5.5 collective-permute-start.4
  16.9 6.7 %collective-permute-done = bf16[2,3,128,512]{3,2,1,0:T(8,128)(2,1)} collective-permute-done((bf16[2,3,128,512]{3,2,1,0:T(8,128)(2,1)}, bf16[2,3,128,512]{3,2,1,0:T(8,128)(2,1)}, u32[]{:S(2)}, u32[]{:S(2)}) %collective-permute-start) | collective-permute-done | bytes 786464 | tf_op jit(solution)/shard_map/ppermute | solution.py:35
  31.0 32.9 %collective-permute-done.4 = bf16[2,3,128,512]{3,2,1,0:T(8,128)(2,1)S(1)} collective-permute-done((bf16[2,3,128,512]{3,2,1,0:T(8,128)(2,1)}, bf16[2,3,128,512]{3,2,1,0:T(8,128)(2,1)S(1)}, u32[]{:S(2)}, u32[]{:S(2)}) %collective-permute-start.4) | collective-permute-done | bytes 786464 | tf_op jit(solution)/shard_map/ppermute | solution.py:35
  64.8 14.4 %collective-permute-done.5 = bf16[2,3,128,512]{3,2,1,0:T(8,128)(2,1)} collective-permute-done((bf16[2,3,128,512]{3,2,1,0:T(8,128)(2,1)}, bf16[2,3,128,512]{3,2,1,0:T(8,128)(2,1)}, u32[]{:S(2)}, u32[]{:S(2)}) %collective-permute-start.5) | collective-permute-done | bytes 786464 | tf_op jit(solution)/shard_map/ppermute | solution.py:35
  81.3 5.6 broadcast_in_dim.107
  86.9 311.9 %while.14 = (s32[]{:T(128)}, f32[2,21,128,512]{3,2,1,0:T(8,128)}, bf16[3,128,512]{2,1,0:T(8,128)(2,1)}, bf16[3,128,512]{2,1,0:T(8,128)(2,1)}, s32[3,16]{1,0:T(4,...) while((s32[]{:T(128)}, f32[2,21,128,512]{3,2,1,0:T(8,128)}, ...), condition=%wide.region_7.9_spmd, body=%wide.region_2.8_spmd.sunk | while | flops 1651705984 | bytes 253007152 | solution.py:136
  86.9 4.8 slice_bitcast_fusion.3
  108.8 4.7 fusion.115
  113.5 4.5 copy.110
  118.1 4.2 reshape.359
  123.3 5.6 multiply_reduce_fusion.3
  134.6 5.8 fusion.119
  147.0 5.3 copy.112
  152.3 4.2 fusion.116
  159.5 5.3 copy.109
  164.7 8.5 %fusion.117 = f32[16,2,128,512]{3,2,1,0:T(8,128)} fusion(f32[1,16,128,512]{3,2,0,1:T(8,128)} %copy.109, f32[1,16,128,512]{3,2,0,1:T(8,128)} %copy.112, pred[16]{0:T(512)(128)(4,1)S(1)} %dynamic-slice_bitcast_fusion.2), kind=kLoop, calls=%fused_computation.14.clone.1 | loop fusion | flops 4194304 | bytes 16777232 | tf_op jit(solution)/shard_map/while/body/eval_jaxpr/jit(_where)/select_n | solution.py:131
  173.3 17.9 %scatter_fusion = f32[2,21,128,512]{3,2,1,0:T(8,128)} fusion(f32[2,21,128,512]{3,2,1,0:T(8,128)} %get-tuple-element.263, s32[16]{0:T(128)S(1)} %fusion.114, f32[16,2,128,512]{3,2,1,0:T(8,128)} %fusion.117), kind=kCustom, calls=%fused_computation.6.clone.1 | custom fusion | flops 2097152 | bytes 25165888 | tf_op jit(solution)/shard_map/while/body/eval_jaxpr/scatter-add | solution.py:132
  191.2 4.8 slice_bitcast_fusion.3
  213.1 4.7 fusion.115
  217.8 4.5 copy.110
  222.3 4.2 reshape.359
  227.6 5.6 multiply_reduce_fusion.3
  238.9 5.8 fusion.119
  251.3 5.3 copy.112
  263.7 5.3 copy.109
  269.0 8.5 %fusion.117 = f32[16,2,128,512]{3,2,1,0:T(8,128)} fusion(f32[1,16,128,512]{3,2,0,1:T(8,128)} %copy.109, f32[1,16,128,512]{3,2,0,1:T(8,128)} %copy.112, pred[16]{0:T(512)(128)(4,1)S(1)} %dynamic-slice_bitcast_fusion.2), kind=kLoop, calls=%fused_computation.14.clone.1 | loop fusion | flops 4194304 | bytes 16777232 | tf_op jit(solution)/shard_map/while/body/eval_jaxpr/jit(_where)/select_n | solution.py:131
  277.5 17.6 %scatter_fusion = f32[2,21,128,512]{3,2,1,0:T(8,128)} fusion(f32[2,21,128,512]{3,2,1,0:T(8,128)} %get-tuple-element.263, s32[16]{0:T(128)S(1)} %fusion.114, f32[16,2,128,512]{3,2,1,0:T(8,128)} %fusion.117), kind=kCustom, calls=%fused_computation.6.clone.1 | custom fusion | flops 2097152 | bytes 25165888 | tf_op jit(solution)/shard_map/while/body/eval_jaxpr/scatter-add | solution.py:132
  295.2 4.8 slice_bitcast_fusion.3
  317.0 4.7 fusion.115
  321.8 4.5 copy.110
  326.3 4.2 reshape.359
  331.6 5.6 multiply_reduce_fusion.3
  342.8 5.8 fusion.119
  355.3 5.3 copy.112
  367.7 5.3 copy.109
  373.0 8.5 %fusion.117 = f32[16,2,128,512]{3,2,1,0:T(8,128)} fusion(f32[1,16,128,512]{3,2,0,1:T(8,128)} %copy.109, f32[1,16,128,512]{3,2,0,1:T(8,128)} %copy.112, pred[16]{0:T(512)(128)(4,1)S(1)} %dynamic-slice_bitcast_fusion.2), kind=kLoop, calls=%fused_computation.14.clone.1 | loop fusion | flops 4194304 | bytes 16777232 | tf_op jit(solution)/shard_map/while/body/eval_jaxpr/jit(_where)/select_n | solution.py:131
  381.5 17.4 %scatter_fusion = f32[2,21,128,512]{3,2,1,0:T(8,128)} fusion(f32[2,21,128,512]{3,2,1,0:T(8,128)} %get-tuple-element.263, s32[16]{0:T(128)S(1)} %fusion.114, f32[16,2,128,512]{3,2,1,0:T(8,128)} %fusion.117), kind=kCustom, calls=%fused_computation.6.clone.1 | custom fusion | flops 2097152 | bytes 25165888 | tf_op jit(solution)/shard_map/while/body/eval_jaxpr/scatter-add | solution.py:132
  398.9 7.4 %fusion.61 = (f32[2,3,128,512]{3,2,1,0:T(8,128)}, f32[2,3,128,512]{3,2,1,0:T(8,128)}, f32[2,3,128,512]{3,2,1,0:T(8,128)}, f32[2,3,128,512]{3,2,1,0:T(8,128)S(1)}...) fusion(f32[2,21,128,512]{3,2,1,0:T(8,128)} %get-tuple-element.60), kind=kLoop, calls=%fused_computation.142 | loop fusion | bytes 18874368 | tf_op jit(solution)/shard_map/slice | solution.py:141
  418.7 4.9 all-to-all-start
  432.6 12.8 %collective-permute-done.13 = bf16[1,2]{1,0:T(2,128)(2,1)} collective-permute-done((bf16[1,2]{1,0:T(2,128)(2,1)S(1)}, bf16[1,2]{1,0:T(2,128)(2,1)}, u32[]{:S(2)}, u32[]{:S(2)}) %collective-permute-start.13) | collective-permute-done | bytes 36 | tf_op jit(solution)/shard_map/ppermute | solution.py:27
  449.7 4.5 collective-permute-start.19
  476.4 5.4 collective-permute-start.6
  481.8 5.9 collective-permute-start.7
  509.2 5.3 all-to-all-start.3
  524.8 56.7 %all-to-all-done.3 = f32[16,2,512]{2,1,0:T(2,128)S(1)} async-done(((f32[16,2,512]{2,1,0:T(2,128)}), f32[16,2,512]{2,1,0:T(2,128)S(1)}, u32[]{:S(2)}, u32[]{:S(2)}) %all-to-all-start.3) | async-done | bytes 65568 | tf_op jit(solution)/shard_map/all_to_all | solution.py:182
  581.4 7.5 %all-to-all-start.2 = ((f32[16,2,512]{2,1,0:T(2,128)}), f32[16,2,512]{2,1,0:T(2,128)S(1)}, u32[]{:S(2)}, u32[]{:S(2)}) async-start(f32[16,2,512]{2,1,0:T(2,128)} %reshape.203), calls=%async_computation.2 | async-start | bytes 131072 | tf_op jit(solution)/shard_map/all_to_all | solution.py:175
  591.5 4.3 all-to-all-done.2
  595.9 5.1 add_add_fusion
  (236 shorter events, 215.2 us)
Async XLA Ops:
  3.1 20.5 %collective-permute-start = (bf16[2,3,128,512]{3,2,1,0:T(8,128)(2,1)}, bf16[2,3,128,512]{3,2,1,0:T(8,128)(2,1)}, u32[]{:S(2)}, u32[]{:S(2)}) collective-permute-start(bf16[2,3,128,512]{3,2,1,0:T(8,128)(2,1)} %get-tuple-element.141), channel_id=1, source_target_pairs={{3,0},{4,1},{5,2},{6,3},{7,4},{8,5},{9,6},{10,7},{11,8},{12,9},{13... | collective-permute-start | bytes 2359304 | tf_op jit(solution)/shard_map/ppermute | solution.py:35
  4.4 23.7 %collective-permute-start.1 = (bf16[2,3,128,512]{3,2,1,0:T(8,128)(2,1)}, bf16[2,3,128,512]{3,2,1,0:T(8,128)(2,1)S(1)}, u32[]{:S(2)}, u32[]{:S(2)}) collective-permute-start(bf16[2,3,128,512]{3,2,1,0:T(8,128)(2,1)} %get-tuple-element.141), channel_id=1, source_target_pairs={{2,0},{3,1},{4,2},{5,3},{6,4},{7,5},{8,6},{9,7},{10,8},{11,9},{12,... | collective-permute-start | bytes 2359304 | tf_op jit(solution)/shard_map/ppermute | solution.py:35
  5.7 23.4 %collective-permute-start.2 = (bf16[2,3,128,512]{3,2,1,0:T(8,128)(2,1)}, bf16[2,3,128,512]{3,2,1,0:T(8,128)(2,1)S(1)}, u32[]{:S(2)}, u32[]{:S(2)}) collective-permute-start(bf16[2,3,128,512]{3,2,1,0:T(8,128)(2,1)} %get-tuple-element.141), channel_id=1, source_target_pairs={{1,0},{2,1},{3,2},{4,3},{5,4},{6,5},{7,6},{8,7},{9,8},{10,9},{11,1... | collective-permute-start | bytes 2359304 | tf_op jit(solution)/shard_map/ppermute | solution.py:35
  7.0 23.0 %collective-permute-start.3 = (bf16[2,3,128,512]{3,2,1,0:T(8,128)(2,1)}, bf16[2,3,128,512]{3,2,1,0:T(8,128)(2,1)S(1)}, u32[]{:S(2)}, u32[]{:S(2)}) collective-permute-start(bf16[2,3,128,512]{3,2,1,0:T(8,128)(2,1)} %get-tuple-element.141), channel_id=1, source_target_pairs={{0,1},{1,2},{2,3},{3,4},{4,5},{5,6},{6,7},{7,8},{8,9},{9,10},{10,1... | collective-permute-start | bytes 2359304 | tf_op jit(solution)/shard_map/ppermute | solution.py:35
  10.1 53.8 %collective-permute-start.4 = (bf16[2,3,128,512]{3,2,1,0:T(8,128)(2,1)}, bf16[2,3,128,512]{3,2,1,0:T(8,128)(2,1)S(1)}, u32[]{:S(2)}, u32[]{:S(2)}) collective-permute-start(bf16[2,3,128,512]{3,2,1,0:T(8,128)(2,1)} %get-tuple-element.141), channel_id=1, source_target_pairs={{0,2},{1,3},{2,4},{3,5},{4,6},{5,7},{6,8},{7,9},{8,10},{9,11},{10,... | collective-permute-start | bytes 2359304 | tf_op jit(solution)/shard_map/ppermute | solution.py:35
  23.6 55.6 %collective-permute-start.5 = (bf16[2,3,128,512]{3,2,1,0:T(8,128)(2,1)}, bf16[2,3,128,512]{3,2,1,0:T(8,128)(2,1)}, u32[]{:S(2)}, u32[]{:S(2)}) collective-permute-start(bf16[2,3,128,512]{3,2,1,0:T(8,128)(2,1)} %get-tuple-element.141), channel_id=1, source_target_pairs={{0,3},{1,4},{2,5},{3,6},{4,7},{5,8},{6,9},{7,10},{8,11},{9,12},{10... | collective-permute-start | bytes 2359304 | tf_op jit(solution)/shard_map/ppermute | solution.py:35
  123.3 5.6 slice-start
  123.3 6.5 %slice-start.1 = ((s8[8388608]{0:T(1024)(128)(4,1)}), s8[4194304]{0:T(1024)(128)(4,1)S(1)}, s32[]{:S(2)}) async-start(s8[8388608]{0:T(1024)(128)(4,1)} %bitcast.154), calls=%async_computation.5 | async-start | bytes 8388608 | tf_op jit(solution)/shard_map/while
  131.0 2.0 copy-start
  227.6 5.6 slice-start
  227.6 6.5 %slice-start.1 = ((s8[8388608]{0:T(1024)(128)(4,1)}), s8[4194304]{0:T(1024)(128)(4,1)S(1)}, s32[]{:S(2)}) async-start(s8[8388608]{0:T(1024)(128)(4,1)} %bitcast.154), calls=%async_computation.5 | async-start | bytes 8388608 | tf_op jit(solution)/shard_map/while
  235.2 2.0 copy-start
  331.6 5.6 slice-start
  331.6 6.5 %slice-start.1 = ((s8[8388608]{0:T(1024)(128)(4,1)}), s8[4194304]{0:T(1024)(128)(4,1)S(1)}, s32[]{:S(2)}) async-start(s8[8388608]{0:T(1024)(128)(4,1)} %bitcast.154), calls=%async_computation.5 | async-start | bytes 8388608 | tf_op jit(solution)/shard_map/while
  339.2 2.0 copy-start
  398.9 8.7 %copy-start.5 = (s32[16]{0:T(128)S(1)}, s32[16]{0:T(128)}, u32[]{:S(2)}) copy-start(s32[16]{0:T(128)} %param.23) | copy-start | bytes 196
  398.9 8.9 %copy-start.6 = (s32[16]{0:T(128)S(1)}, s32[16]{0:T(128)}, u32[]{:S(2)}) copy-start(s32[16]{0:T(128)} %param.22) | copy-start | bytes 196
  398.9 26.4 %copy-start.3 = (bf16[128,512]{1,0:T(8,128)(2,1)S(1)}, bf16[128,512]{1,0:T(8,128)(2,1)}, u32[]{:S(2)}) copy-start(bf16[128,512]{1,0:T(8,128)(2,1)} %param.25) | copy-start | bytes 393220
  398.9 27.2 %copy-start.4 = (bf16[128,512]{1,0:T(8,128)(2,1)S(1)}, bf16[128,512]{1,0:T(8,128)(2,1)}, u32[]{:S(2)}) copy-start(bf16[128,512]{1,0:T(8,128)(2,1)} %param.24) | copy-start | bytes 393220
  406.2 83.9 %collective-permute-start.10 = (f32[2,3,128,512]{3,2,1,0:T(8,128)}, f32[2,3,128,512]{3,2,1,0:T(8,128)S(1)}, u32[]{:S(2)}, u32[]{:S(2)}) collective-permute-start(f32[2,3,128,512]{3,2,1,0:T(8,128)} %get-tuple-element.135), channel_id=1, source_target_pairs={{2,0},{3,1},{4,2},{5,3},{6,4},{7,5},{8,6},{9,7},{10,8},{11,9},{12,... | collective-permute-start | bytes 4718600 | tf_op jit(solution)/shard_map/ppermute | solution.py:35
  408.7 21.5 %collective-permute-start.12 = (bf16[1,2]{1,0:T(2,128)(2,1)S(1)}, bf16[1,2]{1,0:T(2,128)(2,1)}, u32[]{:S(2)}, u32[]{:S(2)}) collective-permute-start(bf16[1,2]{1,0:T(2,128)(2,1)S(1)} %get-tuple-element.157), channel_id=1, source_target_pairs={{0,1},{1,0},{2,3},{3,2},{4,5},{5,4},{6,7},{7,6},{8,9},{9,8},{10,11... | collective-permute-start | bytes 20 | tf_op jit(solution)/shard_map/ppermute | solution.py:27
  408.8 36.5 %collective-permute-start.13 = (bf16[1,2]{1,0:T(2,128)(2,1)S(1)}, bf16[1,2]{1,0:T(2,128)(2,1)}, u32[]{:S(2)}, u32[]{:S(2)}) collective-permute-start(bf16[1,2]{1,0:T(2,128)(2,1)S(1)} %get-tuple-element.156), channel_id=1, source_target_pairs={{0,2},{1,3},{2,0},{3,1},{4,6},{5,7},{6,4},{7,5},{8,10},{9,11},{10,... | collective-permute-start | bytes 20 | tf_op jit(solution)/shard_map/ppermute | solution.py:27
  412.8 35.8 %collective-permute-start.14 = (bf16[1,2]{1,0:T(2,128)(2,1)S(1)}, bf16[1,2]{1,0:T(2,128)(2,1)}, u32[]{:S(2)}, u32[]{:S(2)}) collective-permute-start(bf16[1,2]{1,0:T(2,128)(2,1)S(1)} %get-tuple-element.155), channel_id=1, source_target_pairs={{0,3},{1,2},{2,1},{3,0},{4,7},{5,6},{6,5},{7,4},{8,11},{9,10},{10,... | collective-permute-start | bytes 20 | tf_op jit(solution)/shard_map/ppermute | solution.py:27
  412.8 36.9 %collective-permute-start.15 = (bf16[1,2]{1,0:T(2,128)(2,1)S(1)}, bf16[1,2]{1,0:T(2,128)(2,1)}, u32[]{:S(2)}, u32[]{:S(2)}) collective-permute-start(bf16[1,2]{1,0:T(2,128)(2,1)S(1)} %get-tuple-element.154), channel_id=1, source_target_pairs={{0,4},{1,5},{2,6},{3,7},{4,0},{5,1},{6,2},{7,3},{8,12},{9,13},{10,... | collective-permute-start | bytes 20 | tf_op jit(solution)/shard_map/ppermute | solution.py:27
  418.7 52.0 %all-to-all-start = ((bf16[16,2,512]{2,1,0:T(2,128)(2,1)}), bf16[16,2,512]{2,1,0:T(2,128)(2,1)S(1)}, u32[]{:S(2)}, u32[]{:S(2)}) async-start(bf16[16,2,512]{2,1,0:T(2,128)(2,1)} %reshape.199), calls=%async_computation | async-start | bytes 65536 | tf_op jit(solution)/shard_map/all_to_all | solution.py:165
  426.1 70.0 %copy-start.1 = (bf16[128,512]{0,1:T(8,128)(2,1)}, bf16[128,512]{0,1:T(8,128)(2,1)S(1)}, u32[]{:S(2)}) copy-start(bf16[128,512]{0,1:T(8,128)(2,1)S(1)} %copy.76) | copy-start | bytes 393220
  430.2 24.7 %collective-permute-start.16 = (bf16[1,2]{1,0:T(2,128)(2,1)S(1)}, bf16[1,2]{1,0:T(2,128)(2,1)S(1)}, u32[]{:S(2)}, u32[]{:S(2)}) collective-permute-start(bf16[1,2]{1,0:T(2,128)(2,1)S(1)} %get-tuple-element.153), channel_id=1, source_target_pairs={{0,5},{1,4},{2,7},{3,6},{4,1},{5,0},{6,3},{7,2},{8,13},{9,12},{10,... | collective-permute-start | bytes 20 | tf_op jit(solution)/shard_map/ppermute | solution.py:27
  445.3 9.9 %collective-permute-start.17 = (bf16[1,2]{1,0:T(2,128)(2,1)S(1)}, bf16[1,2]{1,0:T(2,128)(2,1)S(1)}, u32[]{:S(2)}, u32[]{:S(2)}) collective-permute-start(bf16[1,2]{1,0:T(2,128)(2,1)S(1)} %get-tuple-element.152), channel_id=1, source_target_pairs={{0,6},{1,7},{2,4},{3,5},{4,2},{5,3},{6,0},{7,1},{8,14},{9,15},{10,... | collective-permute-start | bytes 20 | tf_op jit(solution)/shard_map/ppermute | solution.py:27
  448.5 8.4 %collective-permute-start.18 = (bf16[1,2]{1,0:T(2,128)(2,1)S(1)}, bf16[1,2]{1,0:T(2,128)(2,1)S(1)}, u32[]{:S(2)}, u32[]{:S(2)}) collective-permute-start(bf16[1,2]{1,0:T(2,128)(2,1)S(1)} %get-tuple-element.151), channel_id=1, source_target_pairs={{0,7},{1,6},{2,5},{3,4},{4,3},{5,2},{6,1},{7,0},{8,15},{9,14},{10,... | collective-permute-start | bytes 20 | tf_op jit(solution)/shard_map/ppermute | solution.py:27
  449.7 9.0 %collective-permute-start.19 = (bf16[1,2]{1,0:T(2,128)(2,1)S(1)}, bf16[1,2]{1,0:T(2,128)(2,1)S(1)}, u32[]{:S(2)}, u32[]{:S(2)}) collective-permute-start(bf16[1,2]{1,0:T(2,128)(2,1)S(1)} %get-tuple-element.150), channel_id=1, source_target_pairs={{0,8},{1,9},{2,10},{3,11},{4,12},{5,13},{6,14},{7,15},{8,0},{9,1},... | collective-permute-start | bytes 20 | tf_op jit(solution)/shard_map/ppermute | solution.py:27
  454.9 5.1 collective-permute-start.20
  455.3 7.5 %collective-permute-start.21 = (bf16[1,2]{1,0:T(2,128)(2,1)S(1)}, bf16[1,2]{1,0:T(2,128)(2,1)S(1)}, u32[]{:S(2)}, u32[]{:S(2)}) collective-permute-start(bf16[1,2]{1,0:T(2,128)(2,1)S(1)} %get-tuple-element.148), channel_id=1, source_target_pairs={{0,10},{1,11},{2,8},{3,9},{4,14},{5,15},{6,12},{7,13},{8,2},{9,3},... | collective-permute-start | bytes 20 | tf_op jit(solution)/shard_map/ppermute | solution.py:27
  457.0 7.9 %collective-permute-start.22 = (bf16[1,2]{1,0:T(2,128)(2,1)S(1)}, bf16[1,2]{1,0:T(2,128)(2,1)S(1)}, u32[]{:S(2)}, u32[]{:S(2)}) collective-permute-start(bf16[1,2]{1,0:T(2,128)(2,1)S(1)} %get-tuple-element.147), channel_id=1, source_target_pairs={{0,11},{1,10},{2,9},{3,8},{4,15},{5,14},{6,13},{7,12},{8,3},{9,2},... | collective-permute-start | bytes 20 | tf_op jit(solution)/shard_map/ppermute | solution.py:27
  458.7 8.4 %collective-permute-start.23 = (bf16[1,2]{1,0:T(2,128)(2,1)S(1)}, bf16[1,2]{1,0:T(2,128)(2,1)S(1)}, u32[]{:S(2)}, u32[]{:S(2)}) collective-permute-start(bf16[1,2]{1,0:T(2,128)(2,1)S(1)} %get-tuple-element.146), channel_id=1, source_target_pairs={{0,12},{1,13},{2,14},{3,15},{4,8},{5,9},{6,10},{7,11},{8,4},{9,5},... | collective-permute-start | bytes 20 | tf_op jit(solution)/shard_map/ppermute | solution.py:27
  460.0 7.1 %collective-permute-start.24 = (bf16[1,2]{1,0:T(2,128)(2,1)S(1)}, bf16[1,2]{1,0:T(2,128)(2,1)S(1)}, u32[]{:S(2)}, u32[]{:S(2)}) collective-permute-start(bf16[1,2]{1,0:T(2,128)(2,1)S(1)} %get-tuple-element.145), channel_id=1, source_target_pairs={{0,13},{1,12},{2,15},{3,14},{4,9},{5,8},{6,11},{7,10},{8,5},{9,4},... | collective-permute-start | bytes 20 | tf_op jit(solution)/shard_map/ppermute | solution.py:27
  462.7 6.3 %collective-permute-start.25 = (bf16[1,2]{1,0:T(2,128)(2,1)S(1)}, bf16[1,2]{1,0:T(2,128)(2,1)S(1)}, u32[]{:S(2)}, u32[]{:S(2)}) collective-permute-start(bf16[1,2]{1,0:T(2,128)(2,1)S(1)} %get-tuple-element.144), channel_id=1, source_target_pairs={{0,14},{1,15},{2,12},{3,13},{4,10},{5,11},{6,8},{7,9},{8,6},{9,7},... | collective-permute-start | bytes 20 | tf_op jit(solution)/shard_map/ppermute | solution.py:27
  464.9 5.7 collective-permute-start.26
  470.7 22.9 %all-to-all-start.1 = ((bf16[16,2,512]{2,1,0:T(2,128)(2,1)}), bf16[16,2,512]{2,1,0:T(2,128)(2,1)S(1)}, u32[]{:S(2)}, u32[]{:S(2)}) async-start(bf16[16,2,512]{2,1,0:T(2,128)(2,1)} %reshape.201), calls=%async_computation.1 | async-start | bytes 65536 | tf_op jit(solution)/shard_map/all_to_all | solution.py:166
  475.1 21.1 %copy-start.2 = (bf16[32,8,64]{0,2,1:T(8,128)(2,1)}, bf16[32,8,64]{0,2,1:T(8,128)(2,1)S(1)}, u32[]{:S(2)}) copy-start(bf16[32,8,64]{0,2,1:T(8,128)(2,1)S(1)} %copy.75) | copy-start | bytes 98308
  475.1 120.8 %collective-permute-start.11 = (f32[2,3,128,512]{3,2,1,0:T(8,128)}, f32[2,3,128,512]{3,2,1,0:T(8,128)}, u32[]{:S(2)}, u32[]{:S(2)}) collective-permute-start(f32[2,3,128,512]{3,2,1,0:T(8,128)} %get-tuple-element.134), channel_id=1, source_target_pairs={{3,0},{4,1},{5,2},{6,3},{7,4},{8,5},{9,6},{10,7},{11,8},{12,9},{13... | collective-permute-start | bytes 4718600 | tf_op jit(solution)/shard_map/ppermute | solution.py:35
  476.4 119.5 %collective-permute-start.6 = (f32[2,3,128,512]{3,2,1,0:T(8,128)}, f32[2,3,128,512]{3,2,1,0:T(8,128)}, u32[]{:S(2)}, u32[]{:S(2)}) collective-permute-start(f32[2,3,128,512]{3,2,1,0:T(8,128)} %get-tuple-element.133), channel_id=1, source_target_pairs={{0,3},{1,4},{2,5},{3,6},{4,7},{5,8},{6,9},{7,10},{8,11},{9,12},{10... | collective-permute-start | bytes 4718600 | tf_op jit(solution)/shard_map/ppermute | solution.py:35
  481.8 114.1 %collective-permute-start.7 = (f32[2,3,128,512]{3,2,1,0:T(8,128)}, f32[2,3,128,512]{3,2,1,0:T(8,128)}, u32[]{:S(2)}, u32[]{:S(2)}) collective-permute-start(f32[2,3,128,512]{3,2,1,0:T(8,128)} %get-tuple-element.138), channel_id=1, source_target_pairs={{0,2},{1,3},{2,4},{3,5},{4,6},{5,7},{6,8},{7,9},{8,10},{9,11},{10,... | collective-permute-start | bytes 4718600 | tf_op jit(solution)/shard_map/ppermute | solution.py:35
  487.7 108.2 %collective-permute-start.8 = (f32[2,3,128,512]{3,2,1,0:T(8,128)}, f32[2,3,128,512]{3,2,1,0:T(8,128)}, u32[]{:S(2)}, u32[]{:S(2)}) collective-permute-start(f32[2,3,128,512]{3,2,1,0:T(8,128)} %get-tuple-element.137), channel_id=1, source_target_pairs={{0,1},{1,2},{2,3},{3,4},{4,5},{5,6},{6,7},{7,8},{8,9},{9,10},{10,1... | collective-permute-start | bytes 4718600 | tf_op jit(solution)/shard_map/ppermute | solution.py:35
  490.2 105.8 %collective-permute-start.9 = (f32[2,3,128,512]{3,2,1,0:T(8,128)S(1)}, f32[2,3,128,512]{3,2,1,0:T(8,128)}, u32[]{:S(2)}, u32[]{:S(2)}) collective-permute-start(f32[2,3,128,512]{3,2,1,0:T(8,128)S(1)} %get-tuple-element.136), channel_id=1, source_target_pairs={{1,0},{2,1},{3,2},{4,3},{5,4},{6,5},{7,6},{8,7},{9,8},{10,9},{11,1... | collective-permute-start | bytes 4718600 | tf_op jit(solution)/shard_map/ppermute | solution.py:35
  509.2 72.2 %all-to-all-start.3 = ((f32[16,2,512]{2,1,0:T(2,128)}), f32[16,2,512]{2,1,0:T(2,128)S(1)}, u32[]{:S(2)}, u32[]{:S(2)}) async-start(f32[16,2,512]{2,1,0:T(2,128)} %reshape.205), calls=%async_computation.3 | async-start | bytes 131072 | tf_op jit(solution)/shard_map/all_to_all | solution.py:182
  581.4 14.4 %all-to-all-start.2 = ((f32[16,2,512]{2,1,0:T(2,128)}), f32[16,2,512]{2,1,0:T(2,128)S(1)}, u32[]{:S(2)}, u32[]{:S(2)}) async-start(f32[16,2,512]{2,1,0:T(2,128)} %reshape.203), calls=%async_computation.2 | async-start | bytes 131072 | tf_op jit(solution)/shard_map/all_to_all | solution.py:175
